TPU v7x, 128 devices: a whole 4x4x4 slice. The times are simulated.
128 devices in a mesh: dp: 4 (over y), pipe: 4 (over z), expert: 8 (over x, core).
Axes of the slice: x: 4, y: 4, z: 4, core: 2. Of those that a mesh axis runs over, the one named last changes fastest.
Arguments:
- tokens: bfloat16 [4, 4096, 5120], P('pipe', ('dp', 'expert')), may hold values from -6 to 6
- cotangent: bfloat16 [4, 4096, 5120], P('pipe', ('dp', 'expert')), may hold values from -6 to 6
- gain: float32 [4, 5120], P('pipe'), may hold values from 0.1 to 1.9
- w_gate: bfloat16 [4, 8, 5120, 768], P('pipe', 'expert', 'dp'), may hold values from -0.078125 to 0.078125
- w_up: bfloat16 [4, 8, 5120, 768], P('pipe', 'expert', 'dp'), may hold values from -0.078125 to 0.078125
- w_down: bfloat16 [4, 8, 768, 5120], P('pipe', 'expert', None, 'dp'), may hold values from -0.21875 to 0.21875
- route: int32 [4, 4, 512, 1], P('pipe', None, ('dp', 'expert')), may hold values from 0 to 7; in each aligned block of 16 rows (0 to 15, 16 to 31, ..., all dimensions but the last counted through in order) at most 3 rows name the same one
Outputs:
- out_tokens: bfloat16 [4, 4096, 5120], P('pipe', ('dp', 'expert'))
- grad_tokens: bfloat16 [4, 4096, 5120], P('pipe', ('dp', 'expert'))
- grad_gain: float32 [4, 5120], P('pipe')
- grad_gate: bfloat16 [4, 8, 5120, 768], P('pipe', 'expert', 'dp')
- grad_up: bfloat16 [4, 8, 5120, 768], P('pipe', 'expert', 'dp')
- grad_down: bfloat16 [4, 8, 768, 5120], P('pipe', 'expert', None, 'dp')
Inputs may be any that keep to these rules, and one draw needn't show every extreme that they name: route[l, m, t, 0] is the expert of tile t at layer l for micro-batch m. Among the 16 tiles of one device for one layer and one micro-batch (aligned blocks), no expert is named more than 3 times; every expert is named somewhere.
All inputs are finite; a program needn't handle non-finite values.
Results may differ from a plain program's by a relative error of at most 0.034.
Values may be sent and summed in bfloat16 or wider, within the bound.
A program may use at most 128 MiB of HBM per device.

v0:
```python
import jax
import jax.numpy as jnp
from jax import lax
from jax.sharding import PartitionSpec as P

TILE = 8
PASSES = 2
epsilon = 1e-06


def shifted(block, axis, distance):
    devices = range(lax.axis_size(axis))
    route = [((i - distance) % len(devices), i) for i in devices]
    return lax.ppermute(block, axis, route)


def contract_last(former, latter):
    return lax.dot_general(
        former, latter, (((1,), (1,)), ((), ())), preferred_element_type=jnp.float32
    )


def contract_first(former, latter):
    return lax.dot_general(
        former, latter, (((0,), (0,)), ((), ())), preferred_element_type=jnp.float32
    )


def normalize(hidden, gain_row):
    widened = hidden.astype(jnp.float32)
    inverse = lax.rsqrt(jnp.mean(widened * widened, axis=-1, keepdims=True) + epsilon)
    scaled = widened * inverse
    return ((scaled * gain_row).astype(jnp.bfloat16), scaled, inverse)


def slot_matrix(route_now, expert_count, capacity):
    tile_count = route_now.shape[0]
    expert_ids = jnp.arange(expert_count, dtype=jnp.int32)
    member = (route_now[None, :] == expert_ids[:, None]).astype(jnp.int32)
    earlier = jnp.cumsum(member, axis=1) - member
    rank_ids = jnp.arange(capacity, dtype=jnp.int32)
    placed = member[:, None, :] * (earlier[:, None, :] == rank_ids[None, :, None]).astype(jnp.int32)
    return placed.reshape(expert_count * capacity, tile_count)


def into_slots(placed, rows, tile_rows, dp_count):
    width = rows.shape[-1]
    tile_blocks = rows.reshape(placed.shape[1], tile_rows, dp_count, width // dp_count)
    return jnp.einsum(
        "st,trqd->qsrd",
        placed.astype(jnp.bfloat16),
        tile_blocks,
        preferred_element_type=jnp.float32,
    ).astype(jnp.bfloat16)


def from_slots(placed, slot_rows):
    merged = jnp.einsum(
        "st,qsrd->trqd", placed.astype(jnp.bfloat16), slot_rows, preferred_element_type=jnp.float32
    ).astype(jnp.bfloat16)
    return merged.reshape(merged.shape[0] * merged.shape[1], -1)


def send_out(slot_rows):
    quarter = slot_rows.shape[-1]
    flat = slot_rows.reshape((-1,) + slot_rows.shape[2:])
    arrived = lax.all_to_all(flat, ("dp", "expert"), split_axis=0, concat_axis=0, tiled=True)
    return arrived.reshape(-1, quarter)


def send_back(part_rows, dp_count, tile_rows):
    quarter = part_rows.shape[-1]
    flat = part_rows.reshape(-1, tile_rows, quarter)
    returned = lax.all_to_all(flat, ("dp", "expert"), split_axis=0, concat_axis=0, tiled=True)
    return returned.reshape(dp_count, -1, tile_rows, quarter)


def widen_rounded(values):
    return lax.optimization_barrier(values.astype(jnp.bfloat16)).astype(jnp.float32)


def expert_forward(received, gate_weight, up_weight, down_weight):
    gate_terms = widen_rounded(jnp.dot(received, gate_weight, preferred_element_type=jnp.float32))
    up_terms = widen_rounded(jnp.dot(received, up_weight, preferred_element_type=jnp.float32))
    gate_pre, up_pre = (
        lax.psum(gate_terms.astype(jnp.bfloat16), "dp").astype(jnp.float32),
        lax.psum(up_terms.astype(jnp.bfloat16), "dp").astype(jnp.float32),
    )
    activated = (jax.nn.silu(gate_pre) * up_pre).astype(jnp.bfloat16)
    part_rows = jnp.dot(activated, down_weight, preferred_element_type=jnp.float32).astype(
        jnp.bfloat16
    )
    return (part_rows, (gate_pre, up_pre, activated))


def expert_backward(
    received, grad_recv, kept_state, gate_weight, up_weight, down_weight, grad_sums
):
    gate_pre, up_pre, activated = kept_state
    grad_terms = widen_rounded(contract_last(grad_recv, down_weight))
    grad_act = lax.psum(grad_terms.astype(jnp.bfloat16), "dp").astype(jnp.float32)
    sigmoid_gate = jax.nn.sigmoid(gate_pre)
    silu_gate = gate_pre * sigmoid_gate
    grad_gate_pre = (
        grad_act * up_pre * sigmoid_gate * (1.0 + gate_pre * (1.0 - sigmoid_gate))
    ).astype(jnp.bfloat16)
    grad_up_pre = (grad_act * silu_gate).astype(jnp.bfloat16)
    back_rows = (
        contract_last(grad_gate_pre, gate_weight) + contract_last(grad_up_pre, up_weight)
    ).astype(jnp.bfloat16)
    grad_gate = grad_sums[0] + contract_first(received, grad_gate_pre)
    grad_up = grad_sums[1] + contract_first(received, grad_up_pre)
    grad_down = grad_sums[2] + contract_first(activated, grad_recv)
    return (back_rows, (grad_gate, grad_up, grad_down))


def body(tokens, cotangent, gain, w_gate, w_up, w_down, route):
    pipe_count = lax.axis_size("pipe")
    dp_count = lax.axis_size("dp")
    expert_count = lax.axis_size("expert")
    section_index = lax.axis_index("pipe")
    gain_row = gain[0]
    gate_weight = w_gate[0, 0]
    up_weight = w_up[0, 0]
    down_weight = w_down[0, 0]
    route_table = route[0, :, :, 0]
    tile_count = route_table.shape[1]
    capacity = max(2, 3 * tile_count // (2 * expert_count))
    hidden = tokens[0]
    saved_ticks = []
    out_rows = hidden
    for pass_index in range(PASSES):
        micro_index = (section_index - pass_index + pipe_count) % pipe_count
        route_now = lax.dynamic_index_in_dim(route_table, micro_index, 0, keepdims=False)
        placed = slot_matrix(route_now, expert_count, capacity)
        normed, scaled, inverse = normalize(hidden, gain_row)
        received = send_out(into_slots(placed, normed, TILE, dp_count))
        part_rows, kept_state = expert_forward(received, gate_weight, up_weight, down_weight)
        ffn_rows = from_slots(placed, send_back(part_rows, dp_count, TILE))
        new_hidden = (hidden.astype(jnp.float32) + ffn_rows.astype(jnp.float32)).astype(
            jnp.bfloat16
        )
        saved_ticks.append((placed, scaled, inverse, received, kept_state))
        if pass_index + 1 < PASSES:
            hidden = shifted(new_hidden, "pipe", 1)
        else:
            out_rows = new_hidden
    grad_rows = cotangent[0]
    grad_sums = (
        jnp.zeros(gate_weight.shape, jnp.float32),
        jnp.zeros(up_weight.shape, jnp.float32),
        jnp.zeros(down_weight.shape, jnp.float32),
    )
    gain_sum = jnp.zeros(gain_row.shape, jnp.float32)
    entry_grad = grad_rows
    for pass_index in reversed(range(PASSES)):
        placed, scaled, inverse, received, kept_state = saved_ticks[pass_index]
        grad_recv = send_out(into_slots(placed, grad_rows, TILE, dp_count))
        back_rows, grad_sums = expert_backward(
            received, grad_recv, kept_state, gate_weight, up_weight, down_weight, grad_sums
        )
        grad_normed = from_slots(placed, send_back(back_rows, dp_count, TILE)).astype(jnp.float32)
        gain_sum = gain_sum + jnp.sum(grad_normed * scaled, axis=0)
        grad_scaled = grad_normed * gain_row
        grad_wide = inverse * (
            grad_scaled - scaled * jnp.mean(grad_scaled * scaled, axis=-1, keepdims=True)
        )
        grad_in = (grad_rows.astype(jnp.float32) + grad_wide).astype(jnp.bfloat16)
        if pass_index > 0:
            grad_rows = shifted(grad_in, "pipe", -1)
        else:
            entry_grad = grad_in
    gain_total = lax.psum(gain_sum, ("dp", "expert"))
    return (
        out_rows[None],
        entry_grad[None],
        gain_total[None],
        grad_sums[0].astype(jnp.bfloat16)[None, None],
        grad_sums[1].astype(jnp.bfloat16)[None, None],
        grad_sums[2].astype(jnp.bfloat16)[None, None],
    )


def solution(mesh):
    placed = (
        P("pipe", ("dp", "expert"), None),
        P("pipe", ("dp", "expert"), None),
        P("pipe", None),
        P("pipe", "expert", "dp", None),
        P("pipe", "expert", "dp", None),
        P("pipe", "expert", None, "dp"),
        P("pipe", None, ("dp", "expert"), None),
    )
    return jax.shard_map(
        body,
        mesh=mesh,
        in_specs=placed,
        out_specs=(
            P("pipe", ("dp", "expert"), None),
            P("pipe", ("dp", "expert"), None),
            P("pipe", None),
            P("pipe", "expert", "dp", None),
            P("pipe", "expert", "dp", None),
            P("pipe", "expert", None, "dp"),
        ),
        check_vma=False,
    )
```

profile of v0, /device:TPU:0, one launch (start us, length us, event | category | flops | bytes accessed | tf_op | source)
XLA Modules:
  0.0 713.0 jit_solution(6603323839218652019)
XLA Ops:
  8.4 1.6 fusion.28
  10.0 1.1 fusion.36
  13.2 34.5 %all_to_all.40 = bf16[96,8,1280]{2,1,0:T(8,128)(2,1)S(1)} all-to-all(bf16[96,8,1280]{2,1,0:T(8,128)(2,1)S(1)} %copy.49), channel_id=1, replica_groups=mesh['dp'=4,'pipe'=4,'expert'=8] {'dp','expert'}, dimensions={0} | all-to-all | bytes 3932160 | tf_op jit(solution)/shard_map/all_to_all | solution.py:67
  47.7 2.7 fusion.94
  50.4 2.7 fusion.99
  53.2 62.0 %all-reduce.10.cloned.1.call-done = (bf16[768,768]{1,0:T(8,128)(2,1)}, bf16[768,768]{1,0:T(8,128)(2,1)}) async-done(((bf16[768,768]{1,0:T(8,128)(2,1)}, bf16[768,768]{1,0:T(8,128)(2,1)}), (bf16[768,768]{1,0:T(8,128)(2,1)}, bf16[768,768]{1,0:T(8,128)(2,1)})) %all-reduce.10.cloned.1.call-update) | async-done | bytes 2359312 | tf_op jit(solution)/shard_map/psum | solution.py:87
  115.2 3.8 fusion.12
  118.9 32.6 %all_to_all.41 = bf16[96,8,1280]{2,1,0:T(8,128)(2,1)S(1)} all-to-all(bf16[96,8,1280]{2,1,0:T(8,128)(2,1)S(1)} %fusion.12), channel_id=1, replica_groups=mesh['dp'=4,'pipe'=4,'expert'=8] {'dp','expert'}, dimensions={0} | all-to-all | bytes 3932160 | tf_op jit(solution)/shard_map/all_to_all | solution.py:74
  152.1 1.7 copy.124
  154.2 1.4 fusion.29
  155.6 2.0 collective-permute-start
  157.8 2.9 convolution_convert_fusion.1
  160.7 2.4 copy.61
  163.1 4.9 all-to-all-start.4
  167.9 20.4 %collective-permute-done = bf16[128,5120]{1,0:T(8,128)(2,1)} collective-permute-done((bf16[128,5120]{1,0:T(8,128)(2,1)}, bf16[128,5120]{1,0:T(8,128)(2,1)}, u32[]{:S(2)}, u32[]{:S(2)}) %collective-permute-start) | collective-permute-done | bytes 1310752 | tf_op jit(solution)/shard_map/ppermute | solution.py:14
  188.4 1.7 fusion.26
  190.0 1.7 fusion.19
  192.7 2.4 copy.55
  195.1 1.3 all-to-all-done.4
  196.4 4.7 all-to-all-start.2
  201.2 4.3 fusion.114
  205.4 24.1 %all-to-all-done.2 = bf16[96,8,1280]{2,1,0:T(8,128)(2,1)} async-done(((bf16[96,8,1280]{2,1,0:T(8,128)(2,1)}), bf16[96,8,1280]{2,1,0:T(8,128)(2,1)}, u32[]{:S(2)}, u32[]{:S(2)}) %all-to-all-start.2) | async-done | bytes 1966112 | tf_op jit(solution)/shard_map/all_to_all | solution.py:67
  229.5 5.0 fusion.104
  234.5 4.3 fusion.109
  238.8 79.5 %all-reduce.8.cloned.1.call-done = (bf16[768,768]{1,0:T(8,128)(2,1)}, bf16[768,768]{1,0:T(8,128)(2,1)}, bf16[768,768]{1,0:T(8,128)(2,1)}) async-done(((bf16[768,768]{1,0:T(8,128)(2,1)}, bf16[768,768]{1,0:T(8,128)(2,1)}, bf16[768,768]{1,0:T(8,128)(2,1)}), (bf16[768,768]{1,0:T(8,128)(2,1)}, bf16[768,768]{1,0:T(8,128)(2,1)}, bf16[768,768]{1,0:T(8,128)(2,1)})) %all-reduce.8.cloned.1.call-update) | async-done | bytes 3538960 | tf_op jit(solution)/shard_map/psum | solution.py:87
  318.3 5.0 fusion.13
  323.4 5.9 all-to-all-start.3
  329.3 5.3 fusion.81
  334.6 3.5 fusion.14
  338.1 19.6 %all-to-all-done.3 = bf16[96,8,1280]{2,1,0:T(8,128)(2,1)} async-done(((bf16[96,8,1280]{2,1,0:T(8,128)(2,1)}), bf16[96,8,1280]{2,1,0:T(8,128)(2,1)}, u32[]{:S(2)}, u32[]{:S(2)}) %all-to-all-start.3) | async-done | bytes 1966112 | tf_op jit(solution)/shard_map/all_to_all | solution.py:74
  357.7 4.7 all-to-all-start.5
  362.5 2.1 fusion.9
  364.6 1.7 copy.123
  366.3 1.9 copy.91
  368.2 22.7 %all-to-all-done.5 = bf16[96,8,1280]{2,1,0:T(8,128)(2,1)} async-done(((bf16[96,8,1280]{2,1,0:T(8,128)(2,1)}), bf16[96,8,1280]{2,1,0:T(8,128)(2,1)}, u32[]{:S(2)}, u32[]{:S(2)}) %all-to-all-start.5) | async-done | bytes 1966112 | tf_op jit(solution)/shard_map/all_to_all | solution.py:74
  390.9 2.1 fusion.7
  393.0 1.7 copy.122
  395.2 2.5 fusion.25
  397.6 3.5 fusion.24
  401.2 2.9 collective-permute-start.1
  404.1 26.3 %collective-permute-done.1 = bf16[128,5120]{1,0:T(8,128)(2,1)} collective-permute-done((bf16[128,5120]{1,0:T(8,128)(2,1)S(1)}, bf16[128,5120]{1,0:T(8,128)(2,1)}, u32[]{:S(2)}, u32[]{:S(2)}) %collective-permute-start.1) | collective-permute-done | bytes 1310752 | tf_op jit(solution)/shard_map/ppermute | solution.py:14
  430.4 3.7 reshape.517
  434.1 2.3 convolution_convert_fusion
  436.4 2.4 copy.67
  438.7 5.3 all-to-all-start.6
  444.6 2.4 reshape.528
  448.3 5.9 fusion.62
  454.2 18.3 %all-to-all-done.6 = bf16[96,8,1280]{2,1,0:T(8,128)(2,1)} async-done(((bf16[96,8,1280]{2,1,0:T(8,128)(2,1)}), bf16[96,8,1280]{2,1,0:T(8,128)(2,1)}, u32[]{:S(2)}, u32[]{:S(2)}) %all-to-all-start.6) | async-done | bytes 1966112 | tf_op jit(solution)/shard_map/all_to_all | solution.py:67
  472.5 4.3 fusion.119
  476.8 6.1 fusion.58
  482.9 5.5 fusion.64
  488.4 33.1 %all-reduce.6.cloned.1.call-done = bf16[768,768]{1,0:T(8,128)(2,1)} async-done(((bf16[768,768]{1,0:T(8,128)(2,1)}), bf16[768,768]{1,0:T(8,128)(2,1)}) %all-reduce.6.cloned.1.call-update) | async-done | bytes 1179664 | tf_op jit(solution)/shard_map/psum | solution.py:101
  521.5 5.3 fusion.79
  526.8 3.5 fusion.15
  530.4 6.8 all-to-all-start.7
  537.3 6.7 fusion.18
  544.0 3.2 fusion.17
  547.2 3.3 fusion.16
  550.5 15.1 %all-to-all-done.7 = bf16[96,8,1280]{2,1,0:T(8,128)(2,1)} async-done(((bf16[96,8,1280]{2,1,0:T(8,128)(2,1)}), bf16[96,8,1280]{2,1,0:T(8,128)(2,1)}, u32[]{:S(2)}, u32[]{:S(2)}) %all-to-all-start.7) | async-done | bytes 1966112 | tf_op jit(solution)/shard_map/all_to_all | solution.py:74
  565.6 5.9 multiply_reduce_fusion
  571.5 125.2 %psum.55 = f32[1,5120]{1,0:T(1,128)} all-reduce(f32[1,5120]{1,0:T(1,128)S(1)} %bitcast.217), channel_id=1, replica_groups=mesh['dp'=4,'pipe'=4,'expert'=8] {'dp','expert'}, use_global_device_ids=true, to_apply=%region_14.15 | all-reduce | flops 5120 | bytes 40960 | tf_op jit(solution)/shard_map/psum | solution.py:173
  696.7 3.4 copy.121
  700.2 2.0 copy.93
  702.3 4.0 fusion.124
  (83 shorter events, 8.1 us)
Async XLA Ops:
  7.2 108.0 %copy-start = (bf16[1,1,768,1280]{3,2,1,0:T(8,128)(2,1)S(1)}, bf16[1,1,768,1280]{3,2,1,0:T(8,128)(2,1)}, u32[]{:S(2)}) copy-start(bf16[1,1,768,1280]{3,2,1,0:T(8,128)(2,1)} %param.12) | copy-start | bytes 5898244
  7.2 2.8 copy-start.1
  7.2 108.0 %all-reduce.10.cloned.1.call-start = ((), (), s32[]{:S(2)}) async-start(), calls=%async_computation.10 | async-start | bytes 4718592 | tf_op jit(solution)/shard_map/psum | solution.py:87
  13.2 34.5 %copy-start.7 = (bf16[1,1,1280,768]{3,2,1,0:T(8,128)(2,1)S(1)}, bf16[1,1,1280,768]{3,2,1,0:T(8,128)(2,1)}, u32[]{:S(2)}) copy-start(bf16[1,1,1280,768]{3,2,1,0:T(8,128)(2,1)} %param.10) | copy-start | bytes 5898244
  47.7 2.7 copy-start.4
  47.7 2.7 copy-start.8
  155.6 32.8 %collective-permute-start = (bf16[128,5120]{1,0:T(8,128)(2,1)}, bf16[128,5120]{1,0:T(8,128)(2,1)}, u32[]{:S(2)}, u32[]{:S(2)}) collective-permute-start(bf16[128,5120]{1,0:T(8,128)(2,1)} %fusion.29), channel_id=1, source_target_pairs={{24,0},{0,8},{8,16},{16,24},{25,1},{1,9},{9,17},{17,25},{26,2},{2,... | collective-permute-start | bytes 3932168 | tf_op jit(solution)/shard_map/ppermute | solution.py:14
  163.1 27.0 %copy-start.6 = (f32[1,5120]{1,0:T(1,128)S(1)}, f32[1,5120]{1,0:T(1,128)}, u32[]{:S(2)}) copy-start(f32[1,5120]{1,0:T(1,128)} %param.9) | copy-start | bytes 61444
  163.1 33.3 %all-to-all-start.4 = ((bf16[96,8,1280]{2,1,0:T(8,128)(2,1)}), bf16[96,8,1280]{2,1,0:T(8,128)(2,1)}, u32[]{:S(2)}, u32[]{:S(2)}) async-start(bf16[96,8,1280]{2,1,0:T(8,128)(2,1)} %copy.61), calls=%async_computation.4 | async-start | bytes 3932160 | tf_op jit(solution)/shard_map/all_to_all | solution.py:67
  196.4 33.2 %all-to-all-start.2 = ((bf16[96,8,1280]{2,1,0:T(8,128)(2,1)}), bf16[96,8,1280]{2,1,0:T(8,128)(2,1)}, u32[]{:S(2)}, u32[]{:S(2)}) async-start(bf16[96,8,1280]{2,1,0:T(8,128)(2,1)} %copy.55), calls=%async_computation.2 | async-start | bytes 3932160 | tf_op jit(solution)/shard_map/all_to_all | solution.py:67
  201.1 117.2 %all-reduce.8.cloned.1.call-start = ((), (), s32[]{:S(2)}) async-start(), calls=%async_computation.9 | async-start | bytes 7077888 | tf_op jit(solution)/shard_map/psum | solution.py:87
  229.5 5.0 copy-start.9
  323.4 34.3 %all-to-all-start.3 = ((bf16[96,8,1280]{2,1,0:T(8,128)(2,1)}), bf16[96,8,1280]{2,1,0:T(8,128)(2,1)}, u32[]{:S(2)}, u32[]{:S(2)}) async-start(bf16[96,8,1280]{2,1,0:T(8,128)(2,1)} %fusion.13), calls=%async_computation.3 | async-start | bytes 3932160 | tf_op jit(solution)/shard_map/all_to_all | solution.py:74
  329.3 5.3 copy-start.10
  329.3 5.3 copy-start.16
  329.3 5.3 copy-start.18
  357.7 33.2 %all-to-all-start.5 = ((bf16[96,8,1280]{2,1,0:T(8,128)(2,1)}), bf16[96,8,1280]{2,1,0:T(8,128)(2,1)}, u32[]{:S(2)}, u32[]{:S(2)}) async-start(bf16[96,8,1280]{2,1,0:T(8,128)(2,1)} %fusion.14), calls=%async_computation.5 | async-start | bytes 3932160 | tf_op jit(solution)/shard_map/all_to_all | solution.py:74
  395.1 2.5 copy-start.2
  395.1 2.5 copy-start.3
  401.2 29.2 %collective-permute-start.1 = (bf16[128,5120]{1,0:T(8,128)(2,1)S(1)}, bf16[128,5120]{1,0:T(8,128)(2,1)}, u32[]{:S(2)}, u32[]{:S(2)}) collective-permute-start(bf16[128,5120]{1,0:T(8,128)(2,1)S(1)} %get-tuple-element.15), channel_id=1, source_target_pairs={{8,0},{16,8},{24,16},{0,24},{9,1},{17,9},{25,17},{1,25},{10,2},{18... | collective-permute-start | bytes 3932168 | tf_op jit(solution)/shard_map/ppermute | solution.py:14
  438.7 33.7 %all-to-all-start.6 = ((bf16[96,8,1280]{2,1,0:T(8,128)(2,1)}), bf16[96,8,1280]{2,1,0:T(8,128)(2,1)}, u32[]{:S(2)}, u32[]{:S(2)}) async-start(bf16[96,8,1280]{2,1,0:T(8,128)(2,1)} %copy.67), calls=%async_computation.6 | async-start | bytes 3932160 | tf_op jit(solution)/shard_map/all_to_all | solution.py:67
  444.0 77.5 %all-reduce.6.cloned.1.call-start = ((), (), s32[]{:S(2)}) async-start(), calls=%async_computation.8 | async-start | bytes 2359296 | tf_op jit(solution)/shard_map/psum | solution.py:101
  476.8 6.2 copy-start.15
  476.8 6.1 copy-start.17
  476.8 6.1 copy-start.19
  521.5 5.3 copy-start.11
  521.5 5.3 copy-start.13
  521.5 5.3 copy-start.20
  530.4 35.3 %all-to-all-start.7 = ((bf16[96,8,1280]{2,1,0:T(8,128)(2,1)}), bf16[96,8,1280]{2,1,0:T(8,128)(2,1)}, u32[]{:S(2)}, u32[]{:S(2)}) async-start(bf16[96,8,1280]{2,1,0:T(8,128)(2,1)} %fusion.15), calls=%async_computation.7 | async-start | bytes 3932160 | tf_op jit(solution)/shard_map/all_to_all | solution.py:74
  537.2 6.8 copy-start.5
  537.2 6.8 copy-start.14
  537.2 6.8 copy-start.21
  537.2 6.8 copy-start.22
  544.0 3.2 copy-start.12
  544.0 3.2 copy-start.23
Sparse Core Ops, SparseCore 0:
  53.3 61.8 all-reduce.9
  238.9 79.3 all-reduce.7
  476.9 44.5 all-reduce.5
where the time goes:
time: 723 us; the launch traced here: 713 us
  waiting for transfers between devices  322 us (45%)
  blocking collectives  192 us (27%)
  matrix products  98 us (14%)
  starting transfers between devices  37.9 us (5%)
  local copies, waits for them, and re-layouts  29.4 us (4%)
  other arithmetic  18.6 us (3%)
  between operations  14.4 us (2%)
    psum x2, waiting for transfers between devices, expert_forward(): lax.psum(up_terms.astype(jnp.bfloat16), 'dp').astype(jnp.float32)  142 us
    psum x1, blocking collectives, body(): gain_total = lax.psum(gain_sum, ('dp', 'expert'))  125 us
    all_to_all x3, waiting for transfers between devices, send_back(): lax.all_to_all(flat, ('dp', 'expert'), split_axis=0, concat_axis=0, tiled...  57.4 us
    ppermute x2, waiting for transfers between devices, shifted(): return lax.ppermute(block, axis, route)  46.7 us
    all_to_all x3, waiting for transfers between devices, send_out(): lax.all_to_all(flat, ('dp', 'expert'), split_axis=0, concat_axis=0, tiled...  43.6 us
    all_to_all x1, blocking collectives, send_out(): lax.all_to_all(flat, ('dp', 'expert'), split_axis=0, concat_axis=0, tiled...  34.5 us
    psum x1, waiting for transfers between devices, expert_backward(): lax.psum(grad_terms.astype(jnp.bfloat16), 'dp').astype(jnp.float32)  33.1 us
    all_to_all x1, blocking collectives, send_back(): lax.all_to_all(flat, ('dp', 'expert'), split_axis=0, concat_axis=0, tiled...  32.6 us
  transfers between devices with their start and end apart: 11, of which 11 were waited for; matrix products, arithmetic and copies ran while one was open for 9% of the time, Pallas kernels for 0%

commit v1 on v0

--- a/solution.py
+++ b/solution.py
@@ -98,7 +98,9 @@
 ):
     gate_pre, up_pre, activated = kept_state
     grad_terms = widen_rounded(contract_last(grad_recv, down_weight))
-    grad_act = lax.psum(grad_terms.astype(jnp.bfloat16), "dp").astype(jnp.float32)
+    grad_act = jnp.sum(lax.all_gather(grad_terms.astype(jnp.bfloat16), "dp"), axis=0).astype(
+        jnp.float32
+    )
     sigmoid_gate = jax.nn.sigmoid(gate_pre)
     silu_gate = gate_pre * sigmoid_gate
     grad_gate_pre = (

time: 723 us -> 781 us (1.080)
  blocking collectives: 192 us -> 224 us
  waiting for transfers between devices: 322 us -> 336 us
  other arithmetic: 18.6 us -> 26.8 us
    all_gather x0 -> x2, waiting for transfers between devices: none -> 93.5 us  [expert_backward(): lax.all_gather(grad_terms.astype(jnp.bfloat16), 'dp')]
    psum x2, waiting for transfers between devices: 142 us -> 106 us  [expert_forward(): lax.psum(up_terms.astype(jnp.bfloat16), 'dp').astype(jnp.float32)]
    psum x1 -> x0, waiting for transfers between devices: 33.1 us -> none  [expert_backward(): lax.psum(grad_terms.astype(jnp.bfloat16), 'dp').astype(jnp.float32)]
    all_to_all x1 -> x2, blocking collectives: 34.5 us -> 66.4 us  [send_out(): lax.all_to_all(flat, ('dp', 'expert'), split_axis=0, concat_axis=0, tiled...]
    all_to_all x3, waiting for transfers between devices: 57.4 us -> 37.4 us  [send_back(): lax.all_to_all(flat, ('dp', 'expert'), split_axis=0, concat_axis=0, tiled...]
    ppermute x2, starting transfers between devices: 4.94 us -> 16.9 us  [shifted(): return lax.ppermute(block, axis, route)]
    ppermute x2, waiting for transfers between devices: 46.7 us -> 56.9 us  [shifted(): return lax.ppermute(block, axis, route)]
    reduce_sum x0 -> x2, other arithmetic: none -> 8.13 us  [expert_backward(): jnp.sum(lax.all_gather(grad_terms.astype(jnp.bfloat16), 'dp'), axis=0)]
  transfers between devices with their start and end apart: 11 -> 11, of which waited for: 11 -> 10; matrix products, arithmetic and copies ran while one was open for 9% -> 10% of each run, Pallas kernels for 0% -> 0%
where the time goes in v1:
time: 781 us; the launch traced here: 771 us
  waiting for transfers between devices  336 us (43%)
  blocking collectives  224 us (29%)
  matrix products  95.4 us (12%)
  starting transfers between devices  44.7 us (6%)
  local copies, waits for them, and re-layouts  29.6 us (4%)
  other arithmetic  26.8 us (3%)
  between operations  14.5 us (2%)
    psum x1, blocking collectives, body(): gain_total = lax.psum(gain_sum, ('dp', 'expert'))  125 us
    psum x2, waiting for transfers between devices, expert_forward(): lax.psum(up_terms.astype(jnp.bfloat16), 'dp').astype(jnp.float32)  106 us
    all_gather x2, waiting for transfers between devices, expert_backward(): lax.all_gather(grad_terms.astype(jnp.bfloat16), 'dp')  93.5 us
    all_to_all x2, blocking collectives, send_out(): lax.all_to_all(flat, ('dp', 'expert'), split_axis=0, concat_axis=0, tiled...  66.4 us
    ppermute x2, waiting for transfers between devices, shifted(): return lax.ppermute(block, axis, route)  56.9 us
    all_to_all x2, waiting for transfers between devices, send_out(): lax.all_to_all(flat, ('dp', 'expert'), split_axis=0, concat_axis=0, tiled...  42.3 us
    all_to_all x3, waiting for transfers between devices, send_back(): lax.all_to_all(flat, ('dp', 'expert'), split_axis=0, concat_axis=0, tiled...  37.4 us
    all_to_all x1, blocking collectives, send_back(): lax.all_to_all(flat, ('dp', 'expert'), split_axis=0, concat_axis=0, tiled...  32.6 us
  transfers between devices with their start and end apart: 11, of which 10 were waited for; matrix products, arithmetic and copies ran while one was open for 10% of the time, Pallas kernels for 0%

profile of v1, /device:TPU:0, one launch (start us, length us, event | category | flops | bytes accessed | tf_op | source)
XLA Modules:
  0.0 771.0 jit_solution(14418199186892424675)
XLA Ops:
  8.4 1.6 fusion.28
  13.2 34.5 %all_to_all.40 = bf16[96,8,1280]{2,1,0:T(8,128)(2,1)S(1)} all-to-all(bf16[96,8,1280]{2,1,0:T(8,128)(2,1)S(1)} %copy.49), channel_id=1, replica_groups=mesh['dp'=4,'pipe'=4,'expert'=8] {'dp','expert'}, dimensions={0} | all-to-all | bytes 3932160 | tf_op jit(solution)/shard_map/all_to_all | solution.py:67
  47.7 2.7 fusion.94
  50.4 2.7 fusion.99
  53.2 62.0 %all-reduce.7.cloned.1.call-done = (bf16[768,768]{1,0:T(8,128)(2,1)}, bf16[768,768]{1,0:T(8,128)(2,1)}) async-done(((bf16[768,768]{1,0:T(8,128)(2,1)}, bf16[768,768]{1,0:T(8,128)(2,1)}), (bf16[768,768]{1,0:T(8,128)(2,1)}, bf16[768,768]{1,0:T(8,128)(2,1)})) %all-reduce.7.cloned.1.call-update) | async-done | bytes 2359312 | tf_op jit(solution)/shard_map/psum | solution.py:87
  115.2 3.8 fusion.12
  118.9 32.6 %all_to_all.41 = bf16[96,8,1280]{2,1,0:T(8,128)(2,1)S(1)} all-to-all(bf16[96,8,1280]{2,1,0:T(8,128)(2,1)S(1)} %fusion.12), channel_id=1, replica_groups=mesh['dp'=4,'pipe'=4,'expert'=8] {'dp','expert'}, dimensions={0} | all-to-all | bytes 3932160 | tf_op jit(solution)/shard_map/all_to_all | solution.py:74
  152.1 1.7 copy.124
  154.2 1.4 fusion.29
  155.6 13.9 %collective-permute-start = (bf16[128,5120]{1,0:T(8,128)(2,1)}, bf16[128,5120]{1,0:T(8,128)(2,1)}, u32[]{:S(2)}, u32[]{:S(2)}) collective-permute-start(bf16[128,5120]{1,0:T(8,128)(2,1)} %fusion.29), channel_id=1, source_target_pairs={{24,0},{0,8},{8,16},{16,24},{25,1},{1,9},{9,17},{17,25},{26,2},{2,... | collective-permute-start | bytes 3932168 | tf_op jit(solution)/shard_map/ppermute | solution.py:14
  169.7 30.6 %collective-permute-done = bf16[128,5120]{1,0:T(8,128)(2,1)} collective-permute-done((bf16[128,5120]{1,0:T(8,128)(2,1)}, bf16[128,5120]{1,0:T(8,128)(2,1)}, u32[]{:S(2)}, u32[]{:S(2)}) %collective-permute-start) | collective-permute-done | bytes 1310752 | tf_op jit(solution)/shard_map/ppermute | solution.py:14
  200.3 1.7 fusion.26
  202.0 1.7 fusion.19
  204.7 2.4 copy.55
  207.0 4.7 all-to-all-start.2
  211.8 2.9 convolution_convert_fusion.1
  214.7 2.4 copy.61
  217.0 23.1 %all-to-all-done.2 = bf16[96,8,1280]{2,1,0:T(8,128)(2,1)} async-done(((bf16[96,8,1280]{2,1,0:T(8,128)(2,1)}), bf16[96,8,1280]{2,1,0:T(8,128)(2,1)}, u32[]{:S(2)}, u32[]{:S(2)}) %all-to-all-start.2) | async-done | bytes 1966112 | tf_op jit(solution)/shard_map/all_to_all | solution.py:67
  240.2 4.7 all-to-all-start.4
  245.0 5.0 fusion.104
  250.0 4.3 fusion.109
  254.3 19.2 %all-to-all-done.4 = bf16[96,8,1280]{2,1,0:T(8,128)(2,1)} async-done(((bf16[96,8,1280]{2,1,0:T(8,128)(2,1)}), bf16[96,8,1280]{2,1,0:T(8,128)(2,1)}, u32[]{:S(2)}, u32[]{:S(2)}) %all-to-all-start.4) | async-done | bytes 1966112 | tf_op jit(solution)/shard_map/all_to_all | solution.py:67
  273.5 4.3 fusion.114
  277.8 43.5 %all-reduce.5.cloned.1.call-done = (bf16[768,768]{1,0:T(8,128)(2,1)}, bf16[768,768]{1,0:T(8,128)(2,1)}) async-done(((bf16[768,768]{1,0:T(8,128)(2,1)}, bf16[768,768]{1,0:T(8,128)(2,1)}), (bf16[768,768]{1,0:T(8,128)(2,1)}, bf16[768,768]{1,0:T(8,128)(2,1)})) %all-reduce.5.cloned.1.call-update) | async-done | bytes 2359312 | tf_op jit(solution)/shard_map/psum | solution.py:87
  321.3 5.0 fusion.13
  326.4 5.7 all-to-all-start.3
  332.1 63.4 %all-gather.5.cloned.1.call-done = bf16[3072,768]{1,0:T(8,128)(2,1)} async-done(((bf16[768,768]{1,0:T(8,128)(2,1)}), bf16[3072,768]{1,0:T(8,128)(2,1)}) %all-gather.5.cloned.1.call-update) | async-done | bytes 4718608 | tf_op jit(solution)/shard_map/all_gather | solution.py:101
  395.5 4.4 reduce_sum.82
  399.9 5.3 fusion.81
  405.2 3.5 fusion.14
  408.7 5.6 all-to-all-start.5
  414.8 2.1 fusion.9
  416.9 1.7 copy.123
  418.6 2.0 copy.91
  420.5 22.2 %all-to-all-done.5 = bf16[96,8,1280]{2,1,0:T(8,128)(2,1)} async-done(((bf16[96,8,1280]{2,1,0:T(8,128)(2,1)}), bf16[96,8,1280]{2,1,0:T(8,128)(2,1)}, u32[]{:S(2)}, u32[]{:S(2)}) %all-to-all-start.5) | async-done | bytes 1966112 | tf_op jit(solution)/shard_map/all_to_all | solution.py:74
  442.7 2.1 fusion.7
  444.8 1.7 copy.122
  447.0 2.5 fusion.25
  449.5 3.5 fusion.24
  453.1 3.0 collective-permute-start.1
  456.0 26.4 %collective-permute-done.1 = bf16[128,5120]{1,0:T(8,128)(2,1)} collective-permute-done((bf16[128,5120]{1,0:T(8,128)(2,1)S(1)}, bf16[128,5120]{1,0:T(8,128)(2,1)}, u32[]{:S(2)}, u32[]{:S(2)}) %collective-permute-start.1) | collective-permute-done | bytes 1310752 | tf_op jit(solution)/shard_map/ppermute | solution.py:14
  482.4 3.7 reshape.517
  486.1 2.3 convolution_convert_fusion
  489.4 31.9 %all_to_all.42 = bf16[96,8,1280]{2,1,0:T(8,128)(2,1)S(1)} all-to-all(bf16[96,8,1280]{2,1,0:T(8,128)(2,1)S(1)} %copy.67), channel_id=1, replica_groups=mesh['dp'=4,'pipe'=4,'expert'=8] {'dp','expert'}, dimensions={0} | all-to-all | bytes 3932160 | tf_op jit(solution)/shard_map/all_to_all | solution.py:67
  521.4 1.3 copy-done.7
  522.6 2.8 fusion.119
  525.5 2.5 reshape.528
  529.3 6.2 fusion.58
  535.5 5.6 fusion.62
  541.1 5.4 fusion.64
  546.6 30.1 %all-gather.7.cloned.1.call-done = bf16[3072,768]{1,0:T(8,128)(2,1)} async-done(((bf16[768,768]{1,0:T(8,128)(2,1)}), bf16[3072,768]{1,0:T(8,128)(2,1)}) %all-gather.7.cloned.1.call-update) | async-done | bytes 4718608 | tf_op jit(solution)/shard_map/all_gather | solution.py:101
  576.6 3.8 reduce_sum.84
  580.4 5.2 fusion.79
  585.7 3.5 fusion.15
  589.2 6.4 all-to-all-start.7
  595.7 6.7 fusion.18
  602.5 3.2 fusion.17
  605.6 3.3 fusion.16
  608.9 15.2 %all-to-all-done.7 = bf16[96,8,1280]{2,1,0:T(8,128)(2,1)S(1)} async-done(((bf16[96,8,1280]{2,1,0:T(8,128)(2,1)}), bf16[96,8,1280]{2,1,0:T(8,128)(2,1)S(1)}, u32[]{:S(2)}, u32[]{:S(2)}) %all-to-all-start.7) | async-done | bytes 1966112 | tf_op jit(solution)/shard_map/all_to_all | solution.py:74
  624.1 5.2 multiply_reduce_fusion
  629.3 125.2 %psum.39 = f32[1,5120]{1,0:T(1,128)} all-reduce(f32[1,5120]{1,0:T(1,128)S(1)} %bitcast.222), channel_id=1, replica_groups=mesh['dp'=4,'pipe'=4,'expert'=8] {'dp','expert'}, use_global_device_ids=true, to_apply=%region_14.15 | all-reduce | flops 5120 | bytes 40960 | tf_op jit(solution)/shard_map/psum | solution.py:175
  754.5 3.4 copy.121
  757.9 2.0 copy.93
  760.1 4.1 fusion.124
  (91 shorter events, 10.3 us)
Async XLA Ops:
  7.2 108.0 %copy-start = (bf16[1,1,768,1280]{3,2,1,0:T(8,128)(2,1)S(1)}, bf16[1,1,768,1280]{3,2,1,0:T(8,128)(2,1)}, u32[]{:S(2)}) copy-start(bf16[1,1,768,1280]{3,2,1,0:T(8,128)(2,1)} %param.12) | copy-start | bytes 5898244
  7.2 2.8 copy-start.2
  7.2 108.0 %all-reduce.7.cloned.1.call-start = ((), (), s32[]{:S(2)}) async-start(), calls=%async_computation.11 | async-start | bytes 4718592 | tf_op jit(solution)/shard_map/psum | solution.py:87
  13.2 34.5 %copy-start.13 = (bf16[1,1,1280,768]{3,2,1,0:T(8,128)(2,1)S(1)}, bf16[1,1,1280,768]{3,2,1,0:T(8,128)(2,1)}, u32[]{:S(2)}) copy-start(bf16[1,1,1280,768]{3,2,1,0:T(8,128)(2,1)} %param.10) | copy-start | bytes 5898244
  47.7 2.7 copy-start.5
  47.7 2.7 copy-start.14
  154.2 47.7 %copy-start.12 = (f32[1,5120]{1,0:T(1,128)S(1)}, f32[1,5120]{1,0:T(1,128)}, u32[]{:S(2)}) copy-start(f32[1,5120]{1,0:T(1,128)} %param.9) | copy-start | bytes 61444
  155.6 44.7 %collective-permute-start = (bf16[128,5120]{1,0:T(8,128)(2,1)}, bf16[128,5120]{1,0:T(8,128)(2,1)}, u32[]{:S(2)}, u32[]{:S(2)}) collective-permute-start(bf16[128,5120]{1,0:T(8,128)(2,1)} %fusion.29), channel_id=1, source_target_pairs={{24,0},{0,8},{8,16},{16,24},{25,1},{1,9},{9,17},{17,25},{26,2},{2,... | collective-permute-start | bytes 3932168 | tf_op jit(solution)/shard_map/ppermute | solution.py:14
  207.0 33.2 %all-to-all-start.2 = ((bf16[96,8,1280]{2,1,0:T(8,128)(2,1)}), bf16[96,8,1280]{2,1,0:T(8,128)(2,1)}, u32[]{:S(2)}, u32[]{:S(2)}) async-start(bf16[96,8,1280]{2,1,0:T(8,128)(2,1)} %copy.55), calls=%async_computation.2 | async-start | bytes 3932160 | tf_op jit(solution)/shard_map/all_to_all | solution.py:67
  240.2 33.3 %all-to-all-start.4 = ((bf16[96,8,1280]{2,1,0:T(8,128)(2,1)}), bf16[96,8,1280]{2,1,0:T(8,128)(2,1)}, u32[]{:S(2)}, u32[]{:S(2)}) async-start(bf16[96,8,1280]{2,1,0:T(8,128)(2,1)} %copy.61), calls=%async_computation.4 | async-start | bytes 3932160 | tf_op jit(solution)/shard_map/all_to_all | solution.py:67
  244.9 76.4 %all-reduce.5.cloned.1.call-start = ((), (), s32[]{:S(2)}) async-start(), calls=%async_computation.10 | async-start | bytes 4718592 | tf_op jit(solution)/shard_map/psum | solution.py:87
  245.0 5.0 copy-start.15
  254.2 141.3 %all-gather.5.cloned.1.call-start = ((), (), s32[]{:S(2)}) async-start(), calls=%async_computation.8 | async-start | bytes 5898240 | tf_op jit(solution)/shard_map/all_gather | solution.py:101
  326.4 82.3 %all-to-all-start.3 = ((bf16[96,8,1280]{2,1,0:T(8,128)(2,1)}), bf16[96,8,1280]{2,1,0:T(8,128)(2,1)}, u32[]{:S(2)}, u32[]{:S(2)}) async-start(bf16[96,8,1280]{2,1,0:T(8,128)(2,1)} %fusion.13), calls=%async_computation.3 | async-start | bytes 3932160 | tf_op jit(solution)/shard_map/all_to_all | solution.py:74
  399.9 5.3 copy-start.8
  399.9 5.3 copy-start.16
  399.9 5.3 copy-start.22
  408.7 34.1 %all-to-all-start.5 = ((bf16[96,8,1280]{2,1,0:T(8,128)(2,1)}), bf16[96,8,1280]{2,1,0:T(8,128)(2,1)}, u32[]{:S(2)}, u32[]{:S(2)}) async-start(bf16[96,8,1280]{2,1,0:T(8,128)(2,1)} %fusion.14), calls=%async_computation.5 | async-start | bytes 3932160 | tf_op jit(solution)/shard_map/all_to_all | solution.py:74
  414.3 162.3 %all-gather.7.cloned.1.call-start = ((), (), s32[]{:S(2)}) async-start(), calls=%async_computation.9 | async-start | bytes 5898240 | tf_op jit(solution)/shard_map/all_gather | solution.py:101
  447.0 2.5 copy-start.3
  447.0 2.5 copy-start.4
  453.1 29.3 %collective-permute-start.1 = (bf16[128,5120]{1,0:T(8,128)(2,1)S(1)}, bf16[128,5120]{1,0:T(8,128)(2,1)}, u32[]{:S(2)}, u32[]{:S(2)}) collective-permute-start(bf16[128,5120]{1,0:T(8,128)(2,1)S(1)} %get-tuple-element.14), channel_id=1, source_target_pairs={{8,0},{16,8},{24,16},{0,24},{9,1},{17,9},{25,17},{1,25},{10,2},{18... | collective-permute-start | bytes 3932168 | tf_op jit(solution)/shard_map/ppermute | solution.py:14
  521.4 1.3 copy-start.7
  529.3 6.2 copy-start.9
  529.3 6.2 copy-start.23
  535.5 5.6 copy-start.21
  580.4 5.3 copy-start.10
  580.4 5.3 copy-start.17
  580.4 5.3 copy-start.19
  589.2 34.9 %all-to-all-start.7 = ((bf16[96,8,1280]{2,1,0:T(8,128)(2,1)}), bf16[96,8,1280]{2,1,0:T(8,128)(2,1)S(1)}, u32[]{:S(2)}, u32[]{:S(2)}) async-start(bf16[96,8,1280]{2,1,0:T(8,128)(2,1)} %fusion.15), calls=%async_computation.7 | async-start | bytes 3932160 | tf_op jit(solution)/shard_map/all_to_all | solution.py:74
  595.6 6.8 copy-start.6
  595.6 6.8 copy-start.11
  595.7 6.8 copy-start.20
  595.7 6.8 copy-start.24
  602.4 3.2 copy-start.18
  602.4 3.2 copy-start.25
  760.0 4.2 copy-start.1
Sparse Core Ops, SparseCore 0:
  53.3 61.8 all-reduce.6
  254.4 66.9 all-reduce.4
  323.6 71.8 all-gather.4
  525.5 51.0 all-gather.6
